TPU v7x, 32 devices: a whole 2x2x4 slice. The times are simulated.
32 devices in a mesh: section: 2 (over y), dp: 4 (over z), ctx: 4 (over x, core).
Axes of the slice: x: 2, y: 2, z: 4, core: 2. Of those that a mesh axis runs over, the one named last changes fastest.
Arguments:
- token_ids: int32 [1024], P('ctx'), may hold values from 0 to 511
- embedding: bfloat16 [512, 4096], P(None, 'dp'), may hold values from -6 to 6
- project_in: bfloat16 [2, 4096, 3, 4096], P('section', 'ctx', None, 'dp'), may hold values from -0.09375 to 0.09375
- short_taps: float32 [2, 3, 3, 4096], P('section', None, None, 'dp'), may hold values from -3.5 to 3.5
- filter_taps: float32 [2, 128, 4096], P('section', None, 'dp'), may hold values from -0.5 to 0.5
- decay_rates: float32 [2, 4096], P('section', 'dp'), may hold values from 0.5 to 4
- project_out: bfloat16 [2, 4096, 4096], P('section', 'dp', 'ctx'), may hold values from -0.09375 to 0.09375
- cotangent: bfloat16 [1024, 4096], P('ctx', 'dp'), may hold values from -0.1875 to 0.1875
Outputs:
- grad_project_in: float32 [2, 4096, 3, 4096], P('section', 'ctx', None, 'dp')
- grad_project_out: float32 [2, 4096, 4096], P('section', 'dp', 'ctx')
- grad_filter: float32 [2, 128, 4096], P('section', None, 'dp')
- grad_decay: float32 [2, 4096], P('section', 'dp')
- grad_short: float32 [2, 3, 3, 4096], P('section', None, None, 'dp')
All inputs are finite; a program needn't handle non-finite values.
Results may differ from a plain program's by a relative error of at most 0.03.
Values may be sent and summed in bfloat16 or wider, within the bound.
No kernel may reach another device: no remote copies, remote signals or barrier semaphores. Data moves between devices by JAX's collectives and lax.ppermute only.
A program may use at most 192 MiB of HBM per device.

v0:
```python
import jax
import jax.numpy as jnp
from jax import lax
from jax.sharding import PartitionSpec as P

EPSILON = 1e-06


def from_behind(value, axis, steps):
    count = lax.axis_size(axis)
    initial, last = (max(0, -steps), min(count, count - steps))
    return lax.ppermute(value, axis, [(source, source + steps) for source in range(initial, last)])


def correlate(signal, kernel):
    channels = signal.shape[1]
    result = lax.conv_general_dilated(
        signal[None],
        kernel[:, None, :],
        (1,),
        "VALID",
        dimension_numbers=("NWC", "WIO", "NWC"),
        feature_group_count=channels,
        precision=lax.Precision.HIGHEST,
    )
    return result[0]


def slice_total(left_rows, right_rows, slice_count):
    row_count = left_rows.shape[0] // slice_count
    slice_parts = jnp.einsum(
        "nsa,nsb->nab",
        left_rows.reshape(slice_count, row_count, -1),
        right_rows.reshape(slice_count, row_count, -1),
        preferred_element_type=jnp.float32,
    )
    return jnp.sum(
        lax.optimization_barrier(slice_parts.astype(jnp.bfloat16)).astype(jnp.float32), axis=0
    )


def local(
    token_ids, embedding, project_in, short_taps, filter_taps, decay_rates, project_out, cotangent
):
    section_zero = lax.axis_index("section") == 0
    tok_rows = token_ids.shape[0]
    local_width = embedding.shape[1]
    weights_in, weights_out = (
        lax.all_gather(project_in[0], "ctx", axis=0, tiled=True),
        lax.all_gather(project_out[0], "ctx", axis=1, tiled=True),
    )
    full_width = weights_in.shape[0]
    chan_count = weights_in.shape[2]
    flat_in = weights_in.reshape(full_width, 3 * chan_count)
    taps_local = short_taps[0]
    filter_local = filter_taps[0]
    tap_count = filter_local.shape[0]
    positions = jnp.arange(tap_count).astype(jnp.float32)
    damping = jnp.exp(-decay_rates[0][None, :] * positions[:, None] / tap_count)
    kernel = filter_local * damping
    onehot = (
        token_ids[:, None] == jnp.arange(embedding.shape[0], dtype=jnp.int32)[None, :]
    ).astype(jnp.bfloat16)
    first_input = jnp.dot(onehot, embedding, preferred_element_type=jnp.float32).astype(
        jnp.bfloat16
    )

    def forward(inputs, apply_out):
        rows_all = lax.all_gather(inputs, "dp", axis=1, tiled=True)
        rows_float = rows_all.astype(jnp.float32)
        inv_rms = lax.rsqrt(jnp.mean(rows_float * rows_float, axis=1, keepdims=True) + EPSILON)
        normed = (rows_float * inv_rms).astype(jnp.bfloat16)
        projected = jnp.dot(normed, flat_in, preferred_element_type=jnp.float32).reshape(
            tok_rows, 3, chan_count
        )
        earlier = from_behind(projected[tok_rows - 2 :], "ctx", 1)
        padded_proj = jnp.concatenate([earlier, projected], axis=0)
        shortened = (
            taps_local[0] * padded_proj[2:]
            + taps_local[1] * padded_proj[1:-1]
            + taps_local[2] * padded_proj[:-2]
        )
        products = shortened[:, 1] * shortened[:, 2]
        earlier_prod = from_behind(
            products[tok_rows - tap_count + 1 :].astype(jnp.bfloat16), "ctx", 1
        ).astype(jnp.float32)
        padded_prod = jnp.concatenate([earlier_prod, products], axis=0)
        filtered = correlate(padded_prod, kernel[::-1])
        gated_rows = (shortened[:, 0] * filtered).astype(jnp.bfloat16)
        saved = (
            inputs,
            rows_float,
            inv_rms,
            normed,
            padded_proj,
            shortened,
            padded_prod,
            filtered,
            gated_rows,
        )
        if apply_out:
            partials = jnp.dot(gated_rows, weights_out, preferred_element_type=jnp.float32)
            summed = lax.psum_scatter(
                partials.astype(jnp.bfloat16), "dp", scatter_dimension=1, tiled=True
            ).astype(jnp.float32)
            return ((inputs.astype(jnp.float32) + summed).astype(jnp.bfloat16), saved)
        return (None, saved)

    def backward(saved, grad_local, need_input):
        (
            inputs,
            rows_float,
            inv_rms,
            normed,
            padded_proj,
            shortened,
            padded_prod,
            filtered,
            gated_rows,
        ) = saved
        grad_rows = lax.all_gather(grad_local, "dp", axis=1, tiled=True)
        grad_gated = lax.dot_general(
            grad_rows, weights_out, (((1,), (1,)), ((), ())), preferred_element_type=jnp.float32
        )
        grad_query = grad_gated * filtered
        grad_filtered = grad_gated * shortened[:, 0]
        later_rows = from_behind(
            grad_filtered[: tap_count - 1].astype(jnp.bfloat16), "ctx", -1
        ).astype(jnp.float32)
        grad_prod = correlate(jnp.concatenate([grad_filtered, later_rows], axis=0), kernel)
        grad_kernel = correlate(padded_prod, grad_filtered)[::-1]
        grad_short_out = jnp.stack(
            [grad_query, grad_prod * shortened[:, 2], grad_prod * shortened[:, 1]], axis=1
        )
        later_short = from_behind(grad_short_out[:2], "ctx", -1)
        padded_short = jnp.concatenate([grad_short_out, later_short], axis=0)
        grad_proj = (
            taps_local[0] * padded_short[:-2]
            + taps_local[1] * padded_short[1:-1]
            + taps_local[2] * padded_short[2:]
        )
        grad_taps = jnp.stack(
            [
                jnp.sum(grad_short_out * padded_proj[2:], axis=0),
                jnp.sum(grad_short_out * padded_proj[1:-1], axis=0),
                jnp.sum(grad_short_out * padded_proj[:-2], axis=0),
            ],
            axis=0,
        )
        grad_proj_b = grad_proj.astype(jnp.bfloat16)
        grad_inputs = None
        if need_input:
            partials = lax.dot_general(
                grad_proj_b.reshape(tok_rows, 3 * chan_count),
                flat_in,
                (((1,), (1,)), ((), ())),
                preferred_element_type=jnp.float32,
            )
            summed_total = lax.psum(partials.astype(jnp.bfloat16), "dp").astype(jnp.float32)
            row_stat = jnp.mean(rows_float * summed_total, axis=1, keepdims=True)
            full_grad = inv_rms * summed_total - rows_float * inv_rms**3 * row_stat
            start_col = lax.axis_index("dp") * local_width
            local_grad = lax.dynamic_slice_in_dim(full_grad, start_col, local_width, 1)
            grad_inputs = (grad_local.astype(jnp.float32) + local_grad).astype(jnp.bfloat16)
        return (grad_inputs, (normed, gated_rows, grad_rows, grad_proj_b, grad_kernel, grad_taps))

    out_first, saved_first = forward(first_input, True)
    arrived = from_behind(out_first, "section", 1)
    unused_out, saved_second = forward(arrived, False)
    back_grad, late_parts = backward(saved_second, cotangent, True)
    returned = from_behind(back_grad, "section", -1)
    unused_grad, early_parts = backward(saved_first, returned, False)
    normed, gated_rows, grad_rows, grad_proj_b, grad_kernel, grad_taps = tuple(
        (
            jnp.where(section_zero, early_item, late_item)
            for early_item, late_item in zip(early_parts, late_parts)
        )
    )
    kernel_sum, taps_sum = (
        lax.psum(grad_kernel.astype(jnp.bfloat16), "ctx").astype(jnp.float32),
        lax.psum(grad_taps.astype(jnp.bfloat16), "ctx").astype(jnp.float32),
    )
    grad_filter = kernel_sum * damping
    grad_decay = (
        -jnp.sum(kernel_sum * filter_local * damping * positions[:, None], axis=0) / tap_count
    )
    flat_grad = grad_proj_b.reshape(tok_rows, 3 * chan_count)
    normed_cols, grad_cols = (
        lax.all_to_all(normed, "ctx", split_axis=1, concat_axis=0, tiled=True),
        lax.all_to_all(grad_rows, "ctx", split_axis=1, concat_axis=0, tiled=True),
    )
    gated_all, flat_all = (
        lax.all_gather(gated_rows, "ctx", axis=0, tiled=True),
        lax.all_gather(flat_grad, "ctx", axis=0, tiled=True),
    )
    slice_count = lax.axis_size("ctx")
    grad_in = slice_total(normed_cols, flat_all, slice_count).reshape(-1, 3, chan_count)
    grad_out = slice_total(gated_all, grad_cols, slice_count)
    return (grad_in[None], grad_out[None], grad_filter[None], grad_decay[None], taps_sum[None])


def solution(mesh):
    return jax.shard_map(
        local,
        mesh=mesh,
        in_specs=(
            P("ctx"),
            P(None, "dp"),
            P("section", "ctx", None, "dp"),
            P("section", None, None, "dp"),
            P("section", None, "dp"),
            P("section", "dp"),
            P("section", "dp", "ctx"),
            P("ctx", "dp"),
        ),
        out_specs=(
            P("section", "ctx", None, "dp"),
            P("section", "dp", "ctx"),
            P("section", None, "dp"),
            P("section", "dp"),
            P("section", None, None, "dp"),
        ),
        check_vma=False,
    )
```

profile of v0, /device:TPU:1, one launch (start us, length us, event | category | flops | bytes accessed | tf_op | source)
XLA Modules:
  0.0 906.4 jit_solution(14686762437870740185)
XLA Ops:
  12.2 46.3 %all-gather.11.cloned.1.call-done = bf16[256,4096]{1,0:T(8,128)(2,1)} async-done(((bf16[256,1024]{1,0:T(8,128)(2,1)}), bf16[256,4096]{1,0:T(8,128)(2,1)}) %all-gather.11.cloned.1.call-update) | async-done | bytes 2097168 | tf_op jit(solution)/shard_map/all_gather | solution.py:69
  60.6 153.5 %all-gather.23.cloned.1.call-done = bf16[1,4096,3,1024]{3,1,2,0:T(8,128)(2,1)} async-done(((bf16[1,1024,3,1024]{3,1,2,0:T(8,128)(2,1)}), bf16[1,4096,3,1024]{3,1,2,0:T(8,128)(2,1)}) %all-gather.23.cloned.1.call-update) | async-done | bytes 25165840 | tf_op jit(solution)/shard_map/all_gather | solution.py:49
  214.1 33.5 %copy.59 = bf16[1,4096,3,1024]{1,3,2,0:T(8,128)(2,1)} copy(bf16[1,4096,3,1024]{3,1,2,0:T(8,128)(2,1)} %all-gather.23.cloned.1.call-done) | data formatting | bytes 50331648 | tf_op jit(solution)/shard_map/all_gather | solution.py:49
  247.6 13.5 %fusion.49 = f32[256,3072]{1,0:T(8,128)} fusion(bf16[4096,3072]{0,1:T(8,128)(2,1)} %bitcast.143, bf16[256,4096]{1,0:T(8,128)(2,1)S(1)} %copy-done.11, f32[256]{0:T(256)S(1)} %add_rsqrt_fusion.1), kind=kOutput, calls=%fused_computation.97 | convolution fusion | flops 6445596672 | bytes 30409728 | tf_op jit(solution)/shard_map/dot_general | solution.py:73
  283.8 10.6 %fusion.62 = f32[1,256,1024]{2,0,1:T(1,128)S(1)} fusion(f32[1,383,1024]{2,0,1:T(1,128)S(1)} %broadcast_in_dim.46, f32[128,1,1024]{2,0,1:T(8,128)S(1)} %bitcast.161), kind=kOutput, calls=%fused_computation.122 | convolution fusion | flops 402653184 | bytes 3141632 | tf_op jit(solution)/shard_map/conv_general_dilated | solution.py:17
  303.1 45.5 %reduce-scatter.2.cloned.1.call-done = bf16[256,1024]{1,0:T(8,128)(2,1)} async-done(((bf16[256,4096]{1,0:T(8,128)(2,1)}), bf16[256,1024]{1,0:T(8,128)(2,1)}) %reduce-scatter.2.cloned.1.call-update) | async-done | bytes 524304 | tf_op jit(solution)/shard_map/reduce_scatter | solution.py:103
  364.8 47.0 %all-gather.13.cloned.1.call-done = bf16[256,4096]{1,0:T(8,128)(2,1)} async-done(((bf16[256,1024]{1,0:T(8,128)(2,1)}), bf16[256,4096]{1,0:T(8,128)(2,1)}) %all-gather.13.cloned.1.call-update) | async-done | bytes 2097168 | tf_op jit(solution)/shard_map/all_gather | solution.py:69
  413.9 13.9 %fusion.48 = f32[256,3072]{1,0:T(8,128)} fusion(bf16[4096,3072]{0,1:T(8,128)(2,1)} %bitcast.144, bf16[256,4096]{1,0:T(8,128)(2,1)} %all-gather.13.cloned.1.call-done, f32[256]{0:T(256)S(1)} %get-tuple-element.36), kind=kOutput, calls=%fused_computation.96 | convolution fusion | flops 6445596672 | bytes 30409728 | tf_op jit(solution)/shard_map/dot_general | solution.py:73
  447.0 11.0 %all-gather.15.cloned.1.call-done = bf16[256,4096]{1,0:T(8,128)(2,1)} async-done(((bf16[256,1024]{1,0:T(8,128)(2,1)}), bf16[256,4096]{1,0:T(8,128)(2,1)}) %all-gather.15.cloned.1.call-update) | async-done | bytes 2097168 | tf_op jit(solution)/shard_map/all_gather | solution.py:121
  472.6 10.6 %fusion.32 = f32[1,256,1024]{2,0,1:T(1,128)S(1)} fusion(f32[1,383,1024]{2,1,0:T(8,128)S(1)} %maximum_bitcast_fusion.1, f32[128,1,1024]{2,0,1:T(8,128)S(1)} %bitcast_multiply_fusion.8), kind=kOutput, calls=%fused_computation.64 | convolution fusion | flops 402653184 | bytes 3141632 | tf_op jit(solution)/shard_map/conv_general_dilated | solution.py:17
  489.3 10.6 %fusion.52 = f32[1,256,1024]{2,0,1:T(1,128)S(1)} fusion(f32[1,383,1024]{2,1,0:T(8,128)S(1)} %maximum_bitcast_fusion, f32[128,1,1024]{2,0,1:T(8,128)S(1)} %bitcast.162), kind=kOutput, calls=%fused_computation.99 | convolution fusion | flops 402653184 | bytes 3141632 | tf_op jit(solution)/shard_map/conv_general_dilated | solution.py:17
  511.0 13.2 %fusion.11 = bf16[256,4096]{1,0:T(8,128)(2,1)} fusion(bf16[256,3,1024]{2,0,1:T(8,128)(2,1)S(1)} %get-tuple-element.24, bf16[1,4096,3,1024]{3,1,2,0:T(8,128)(2,1)} %all-gather.23.cloned.1.call-done), kind=kOutput, calls=%fused_computation.15 | convolution fusion | flops 6443499520 | bytes 28835840 | tf_op jit(solution)/shard_map/dot_general | solution.py:153
  531.1 77.2 %all-reduce.3.cloned.1.call-done = bf16[256,4096]{1,0:T(8,128)(2,1)} async-done(((bf16[256,4096]{1,0:T(8,128)(2,1)}), bf16[256,4096]{1,0:T(8,128)(2,1)}) %all-reduce.3.cloned.1.call-update) | async-done | bytes 2097168 | tf_op jit(solution)/shard_map/psum | solution.py:159
  614.6 13.4 %collective-permute-done.7 = bf16[256,1024]{1,0:T(8,128)(2,1)S(1)} collective-permute-done((bf16[256,1024]{1,0:T(8,128)(2,1)S(1)}, bf16[256,1024]{1,0:T(8,128)(2,1)S(1)}, u32[]{:S(2)}, u32[]{:S(2)}) %collective-permute-start.7) | collective-permute-done | bytes 524320 | tf_op jit(solution)/shard_map/ppermute | solution.py:12
  628.9 12.1 %fusion.42 = bf16[1,128,1024]{2,0,1:T(2,128)(2,1)S(1)} fusion(f32[256,1,1024]{2,0,1:T(8,128)S(1)} %bitcast.157, f32[1,383,1024]{2,1,0:T(8,128)} %copy-done.26), kind=kOutput, calls=%fused_computation.87 | convolution fusion | flops 402653184 | bytes 2879488 | tf_op jit(solution)/shard_map/conv_general_dilated | solution.py:17
  641.4 32.6 %all-gather.17.cloned.1.call-done = bf16[256,4096]{1,0:T(8,128)(2,1)} async-done(((bf16[256,1024]{1,0:T(8,128)(2,1)}), bf16[256,4096]{1,0:T(8,128)(2,1)}) %all-gather.17.cloned.1.call-update) | async-done | bytes 2097168 | tf_op jit(solution)/shard_map/all_gather | solution.py:121
  684.5 10.5 %fusion.44 = bf16[1,128,1024]{2,0,1:T(2,128)(2,1)S(1)} fusion(f32[1,383,1024]{2,0,1:T(1,128)S(1)} %copy-done.28, f32[256,1,1024]{2,0,1:T(8,128)S(1)} %bitcast.158), kind=kOutput, calls=%fused_computation.89 | convolution fusion | flops 402653184 | bytes 2879488 | tf_op jit(solution)/shard_map/conv_general_dilated | solution.py:17
  701.2 10.6 %fusion.30 = f32[1,256,1024]{2,0,1:T(1,128)S(1)} fusion(f32[1,383,1024]{2,1,0:T(8,128)S(1)} %maximum_bitcast_fusion.2, f32[128,1,1024]{2,0,1:T(8,128)S(1)} %copy-done.34), kind=kOutput, calls=%fused_computation.62 | convolution fusion | flops 402653184 | bytes 3141632 | tf_op jit(solution)/shard_map/conv_general_dilated | solution.py:17
  749.7 17.6 %all-to-all-done.1 = bf16[256,4,1024]{2,0,1:T(8,128)(2,1)S(1)} async-done(((bf16[256,4,1024]{2,0,1:T(8,128)(2,1)}), bf16[256,4,1024]{2,0,1:T(8,128)(2,1)S(1)}, u32[]{:S(2)}, u32[]{:S(2)}) %all-to-all-start.1) | async-done | bytes 2097184 | tf_op jit(solution)/shard_map/all_to_all | solution.py:190
  784.2 43.0 %psum.23 = bf16[1,3,3,1024]{3,2,1,0:T(4,128)(2,1)S(1)} all-reduce(bf16[1,3,3,1024]{3,2,1,0:T(4,128)(2,1)S(1)} %fusion.68), channel_id=1, replica_groups=mesh['section'=2,'dp'=4,'ctx'=4] {'ctx'}, use_global_device_ids=true, to_apply=%region_15.16 | all-reduce | flops 9216 | bytes 36864 | tf_op jit(solution)/shard_map/psum | solution.py:181
  844.5 14.9 %convolution_convert_fusion = bf16[4,1024,3072]{2,1,0:T(8,128)(2,1)} fusion(bf16[4,256,3072]{2,1,0:T(8,128)(2,1)} %bitcast.145, bf16[256,4,1024]{0,2,1:T(8,128)(2,1)} %all-to-all-done), kind=kOutput, calls=%fused_computation.3 | convolution fusion | flops 6455033856 | bytes 33554432 | tf_op jit(solution)/shard_map/nsa,nsb->nab/dot_general | solution.py:31
  859.4 14.6 %convert_reduce_fusion = f32[1024,3072]{1,0:T(8,128)} fusion(bf16[4,1024,3072]{2,1,0:T(8,128)(2,1)} %convolution_convert_fusion), kind=kLoop, calls=%fused_computation | loop fusion | flops 22020096 | bytes 37748736 | tf_op jit(solution)/shard_map/reduce_sum | solution.py:37
  874.0 12.7 %copy.77 = f32[1024,3072]{0,1:T(8,128)} copy(f32[1024,3072]{1,0:T(8,128)} %convert_reduce_fusion) | data formatting | bytes 25165824 | tf_op jit(solution)/shard_map/reduce_sum | solution.py:37
  886.7 12.7 %copy.87 = f32[1,1024,3,1024]{3,1,2,0:T(8,128)} copy(f32[1,1024,3,1024]{1,3,2,0:T(8,128)} %bitcast.142) | data formatting | bytes 25165824
  (220 shorter events, 210.0 us)
Async XLA Ops:
  7.2 51.3 %all-gather.11.cloned.1.call-start = ((), (), s32[]{:S(2)}) async-start(), calls=%async_computation.3 | async-start | bytes 2621440 | tf_op jit(solution)/shard_map/all_gather | solution.py:69
  10.4 203.7 %all-gather.23.cloned.1.call-start = ((), (), s32[]{:S(2)}) async-start(), calls=%async_computation.12 | async-start | bytes 31457280 | tf_op jit(solution)/shard_map/all_gather | solution.py:49
  11.2 284.6 %all-gather.25.cloned.1.call-start = ((), (), s32[]{:S(2)}) async-start(), calls=%async_computation.13 | async-start | bytes 10485760 | tf_op jit(solution)/shard_map/all_gather | solution.py:50
  11.9 336.7 %reduce-scatter.2.cloned.1.call-start = ((), (), s32[]{:S(2)}) async-start(), calls=%async_computation.4 | async-start | bytes 2621440 | tf_op jit(solution)/shard_map/reduce_scatter | solution.py:103
  12.0 455.3 %copy-start.37 = (f32[1,1024]{1,0:T(1,128)}, f32[1,1024]{1,0:T(1,128)S(1)}, u32[]{:S(2)}) copy-start(f32[1,1024]{1,0:T(1,128)S(1)} %neg.14) | copy-start | bytes 12292
  262.0 9.6 %collective-permute-start = (f32[2,3,1024]{2,0,1:T(2,128)S(1)}, f32[2,3,1024]{2,0,1:T(2,128)S(1)}, u32[]{:S(2)}, u32[]{:S(2)}) collective-permute-start(f32[2,3,1024]{2,0,1:T(2,128)S(1)} %bitcast.174), channel_id=1, source_target_pairs={{0,1},{1,2},{2,3},{4,5},{5,6},{6,7},{8,9},{9,10},{10,11},{12,13},{... | collective-permute-start | bytes 73736 | tf_op jit(solution)/shard_map/ppermute | solution.py:12
  277.1 5.4 collective-permute-start.1
  303.1 108.8 %all-gather.13.cloned.1.call-start = ((), (), s32[]{:S(2)}) async-start(), calls=%async_computation.5 | async-start | bytes 2621440 | tf_op jit(solution)/shard_map/all_gather | solution.py:69
  349.9 13.5 %collective-permute-start.2 = (bf16[256,1024]{1,0:T(8,128)(2,1)S(1)}, bf16[256,1024]{1,0:T(8,128)(2,1)S(1)}, u32[]{:S(2)}, u32[]{:S(2)}) collective-permute-start(bf16[256,1024]{1,0:T(8,128)(2,1)S(1)} %add_convert_fusion), channel_id=1, source_target_pairs={{0,16},{1,17},{2,18},{3,19},{4,20},{5,21},{6,22},{7,23},{8,24},{9,... | collective-permute-start | bytes 1572872 | tf_op jit(solution)/shard_map/ppermute | solution.py:12
  364.2 93.8 %all-gather.15.cloned.1.call-start = ((), (), s32[]{:S(2)}) async-start(), calls=%async_computation.6 | async-start | bytes 2621440 | tf_op jit(solution)/shard_map/all_gather | solution.py:121
  364.8 243.6 %all-reduce.3.cloned.1.call-start = ((), (), s32[]{:S(2)}) async-start(), calls=%async_computation.7 | async-start | bytes 4194304 | tf_op jit(solution)/shard_map/psum | solution.py:159
  428.8 11.2 %collective-permute-start.3 = (f32[2,3,1024]{2,0,1:T(2,128)S(1)}, f32[2,3,1024]{2,0,1:T(2,128)S(1)}, u32[]{:S(2)}, u32[]{:S(2)}) collective-permute-start(f32[2,3,1024]{2,0,1:T(2,128)S(1)} %bitcast.175), channel_id=1, source_target_pairs={{0,1},{1,2},{2,3},{4,5},{5,6},{6,7},{8,9},{9,10},{10,11},{12,13},{... | collective-permute-start | bytes 73736 | tf_op jit(solution)/shard_map/ppermute | solution.py:12
  464.6 7.7 collective-permute-start.5
  483.8 5.2 collective-permute-start.4
  501.2 6.3 collective-permute-start.6
  524.2 149.8 %all-gather.17.cloned.1.call-start = ((), (), s32[]{:S(2)}) async-start(), calls=%async_computation.8 | async-start | bytes 2621440 | tf_op jit(solution)/shard_map/all_gather | solution.py:121
  613.3 14.7 %collective-permute-start.7 = (bf16[256,1024]{1,0:T(8,128)(2,1)S(1)}, bf16[256,1024]{1,0:T(8,128)(2,1)S(1)}, u32[]{:S(2)}, u32[]{:S(2)}) collective-permute-start(bf16[256,1024]{1,0:T(8,128)(2,1)S(1)} %fusion.36), channel_id=1, source_target_pairs={{16,0},{17,1},{18,2},{19,3},{20,4},{21,5},{22,6},{23,7},{24,8},{25... | collective-permute-start | bytes 1572872 | tf_op jit(solution)/shard_map/ppermute | solution.py:12
  628.8 118.8 %all-reduce.5.cloned.1.call-start = ((), (), s32[]{:S(2)}) async-start(), calls=%async_computation.11 | async-start | bytes 524288 | tf_op jit(solution)/shard_map/psum | solution.py:180
  681.6 17.2 %collective-permute-start.8 = (bf16[127,1024]{1,0:T(8,128)(2,1)}, bf16[127,1024]{1,0:T(8,128)(2,1)}, u32[]{:S(2)}, u32[]{:S(2)}) collective-permute-start(bf16[127,1024]{1,0:T(8,128)(2,1)} %slice.238), channel_id=1, source_target_pairs={{1,0},{2,1},{3,2},{5,4},{6,5},{7,6},{9,8},{10,9},{11,10},{13,12},{... | collective-permute-start | bytes 780296 | tf_op jit(solution)/shard_map/ppermute | solution.py:12
  696.3 131.6 %all-gather.21.cloned.1.call-start = ((), (), s32[]{:S(2)}) async-start(), calls=%async_computation.10 | async-start | bytes 2621440 | tf_op jit(solution)/shard_map/all_gather | solution.py:193
  698.8 137.1 %all-gather.19.cloned.1.call-start = ((), (), s32[]{:S(2)}) async-start(), calls=%async_computation.9 | async-start | bytes 7864320 | tf_op jit(solution)/shard_map/all_gather | solution.py:194
  714.9 5.8 collective-permute-start.9
  729.4 37.8 %all-to-all-start.1 = ((bf16[256,4,1024]{2,0,1:T(8,128)(2,1)}), bf16[256,4,1024]{2,0,1:T(8,128)(2,1)S(1)}, u32[]{:S(2)}, u32[]{:S(2)}) async-start(bf16[256,4,1024]{2,0,1:T(8,128)(2,1)} %bitcast.152), calls=%async_computation.2 | async-start | bytes 4194304 | tf_op jit(solution)/shard_map/all_to_all | solution.py:190
  767.3 77.3 %all-to-all-start = ((bf16[256,4,1024]{0,2,1:T(8,128)(2,1)}), bf16[256,4,1024]{0,2,1:T(8,128)(2,1)}, u32[]{:S(2)}, u32[]{:S(2)}) async-start(bf16[256,4,1024]{0,2,1:T(8,128)(2,1)} %bitcast.151), calls=%async_computation.1 | async-start | bytes 4194304 | tf_op jit(solution)/shard_map/all_to_all | solution.py:189
  (44 other events, 1174.2 us)
Sparse Core Ops, SparseCore 0:
  10.5 47.9 all-gather.10
  60.1 153.9 all-gather.22
  215.7 58.2 all-gather.24
  303.2 45.3 reduce-scatter.1
  364.3 47.4 all-gather.12
  413.3 44.6 all-gather.14
  524.3 83.9 all-reduce.2
  628.9 45.0 all-gather.16
  696.4 29.3 all-reduce.4
  727.2 35.8 all-gather.20
  764.7 70.0 all-gather.18
where the time goes:
time: 915 us; the launch traced here: 906 us
  waiting for transfers between devices  475 us (52%)
  matrix products  147 us (16%)
  local copies, waits for them, and re-layouts  120 us (13%)
  other arithmetic  71.7 us (8%)
  blocking collectives  43 us (5%)
  starting transfers between devices  34.6 us (4%)
  between operations  15.3 us (2%)
    all_gather x1, waiting for transfers between devices, local(): lax.all_gather(project_in[0], 'ctx', axis=0, tiled=True)  153 us
    all_gather x2, waiting for transfers between devices, forward(): rows_all = lax.all_gather(inputs, 'dp', axis=1, tiled=True)  93.3 us
    psum x1, waiting for transfers between devices, backward(): lax.psum(partials.astype(jnp.bfloat16), 'dp').astype(jnp.float32)  77.2 us
    conv_general_dilated x6, matrix products, correlate(): lax.conv_general_dilated(signal[None], kernel[:, None, :], (1,), 'VALID',...  65 us
    reduce_scatter x1, waiting for transfers between devices, forward(): lax.psum_scatter(partials.astype(jnp.bfloat16), 'dp', scatter_dimension=1...  45.5 us
    all_gather x2, waiting for transfers between devices, backward(): grad_rows = lax.all_gather(grad_local, 'dp', axis=1, tiled=True)  43.6 us
    psum x1, blocking collectives, local(): lax.psum(grad_taps.astype(jnp.bfloat16), 'ctx').astype(jnp.float32)  43 us
    ppermute x10, waiting for transfers between devices, from_behind(): lax.ppermute(value, axis, [(source, source + steps) for source in range(i...  42.1 us
  transfers between devices with their start and end apart: 23, of which 15 were waited for; matrix products, arithmetic and copies ran while one was open for 23% of the time, Pallas kernels for 0%

commit v1 on v0

v1 whole, which is shorter than its diff:
```python
import functools

import jax
import jax.numpy as jnp
import numpy as np
from jax import lax
from jax.experimental import pallas as pl
from jax.experimental.pallas import tpu as pltpu
from jax.sharding import PartitionSpec as P

EPSILON = 1e-06
F32 = jnp.float32
BF16 = jnp.bfloat16


def dot(left, right):
    return jnp.dot(left, right, preferred_element_type=F32)


def dot_t(left, right):
    return lax.dot_general(left, right, (((1,), (1,)), ((), ())), preferred_element_type=F32)


def exact(left, right):
    return jnp.dot(left, right, preferred_element_type=F32, precision=lax.Precision.HIGHEST)


def pick(stack, index):
    return lax.dynamic_index_in_dim(stack, index, 0, keepdims=False)


def send(value, axes, route):
    sizes = [lax.axis_size(axis) for axis in axes]
    pairs = []
    for source, place in enumerate(np.ndindex(*sizes)):
        target = route(*place)
        if target is not None:
            pairs.append((source, int(np.ravel_multi_index(target, sizes))))
    return lax.ppermute(value, axes, pairs)


def ctx_xor(value, mask, sections):
    return send(
        value, ("section", "ctx"), lambda s, k: (s, k ^ mask) if s in sections else None
    )


def ctx_gather(value, sections):
    count = lax.axis_size("ctx")
    held = {0: value}
    bit = count // 2
    while bit:
        for r in list(held):
            held[r | bit] = ctx_xor(held[r], bit, sections)
        bit //= 2
    return [held[r] for r in range(count)]


def scatter_order(count):
    if count == 1:
        return [0]
    inner = scatter_order(count // 2)
    return [2 * r for r in inner] + [2 * r + 1 for r in inner]


def dp_gather(value, section, parts):
    count = lax.axis_size("dp")
    pieces = [jnp.split(value, parts, axis=0)]
    for _ in range(count - 1):
        pieces.append(
            [
                send(
                    piece,
                    ("section", "dp"),
                    lambda s, z: (s, (z + 1) % count) if s == section else None,
                )
                for piece in pieces[-1]
            ]
        )
    return jnp.stack([jnp.concatenate(piece, axis=0) for piece in pieces])


def cross_sum(shares, source):
    count = lax.axis_size("dp")
    me = lax.axis_index("dp")
    total = 0.0
    for shift in range(count):
        arrived = send(
            pick(shares, (me + shift) % count),
            ("section", "dp"),
            lambda s, z: (1 - s, (z + shift) % count) if s == source else None,
        )
        total = total + arrived.astype(F32)
    return total


def in_order(stack, me):
    return [pick(stack, (me - q) % stack.shape[0]) for q in range(stack.shape[0])]


def spectra(taps):
    freq = np.arange(taps)[:, None]
    time = np.arange(taps)[None, :]
    angle = np.pi * freq * time / taps
    nyquist = np.where(time % 2 == 0, 1.0, -1.0)
    forward = np.concatenate(
        [np.cos(angle), np.where(freq == 0, nyquist, -np.sin(angle))], axis=0
    )
    weight = np.where(freq == 0, 1.0, 2.0) / (2 * taps)
    inverse = np.concatenate(
        [weight * np.cos(angle), np.where(freq == 0, nyquist, -2 * np.sin(angle)) * np.where(freq == 0, weight, 1.0 / (2 * taps))],
        axis=0,
    ).T
    sign = np.where(np.arange(2 * taps) % taps % 2 == 0, 1.0, -1.0)
    return [jnp.asarray(m, BF16) for m in (forward, inverse, inverse * sign[None, :])]


def later(current, before, steps, row):
    return jnp.where(row < steps, pltpu.roll(before, steps, 0), pltpu.roll(current, steps, 0))


def sooner(current, after, steps, row):
    count = current.shape[0]
    return jnp.where(
        row >= count - steps,
        pltpu.roll(after, count - steps, 0),
        pltpu.roll(current, count - steps, 0),
    )


def kernel_spectrum(fwd_ref, kern_ref, row):
    tap_count = kern_ref.shape[0]
    kern = dot(fwd_ref[...], kern_ref[...].astype(BF16))
    real, imag = kern[:tap_count], kern[tap_count:]
    return real, jnp.where(row == 0, 0.0, imag), jnp.where(row == 0, imag, real)


def proj_block(proj_ref, m, b, tap_count):
    chunk, start = divmod(b * tap_count, proj_ref.shape[2])
    return proj_ref[chunk, m, start : start + tap_count, :].astype(F32)


def short_filter(taps_ref, m, current, before, row):
    return (
        taps_ref[m : m + 1, :] * current
        + taps_ref[3 + m : 4 + m, :] * later(current, before, 1, row)
        + taps_ref[6 + m : 7 + m, :] * later(current, before, 2, row)
    )


def lookup_kernel(
    tokens_ref, table_ref, taps_ref, kern_ref, fwd_ref, inv_ref,
    gated_ref, filt_ref, spec_ref, proj_ref,
):
    tap_count, vocab = kern_ref.shape[0], table_ref.shape[1]
    entry = lax.broadcasted_iota(jnp.int32, (tap_count, vocab), 1)
    for b in range(filt_ref.shape[0] // tap_count):
        here = pl.ds(b * tap_count, tap_count)
        chosen = (entry == tokens_ref[here, :]).astype(F32).astype(BF16)
        for m in range(3):
            proj_ref[0, m, here, :] = dot(chosen, table_ref[m]).astype(BF16)
    forward_kernel(
        proj_ref, taps_ref, kern_ref, fwd_ref, inv_ref, gated_ref, filt_ref, spec_ref
    )


def collect_kernel(
    tokens_ref, scale_ref, gg_ref, proj_ref, taps_ref, kern_ref, fwd_ref, inv_ref, filt_ref, spec_ref,
    table_ref, gkern_ref, gtaps_ref, grad_spec, gproj_ref,
):
    backward_kernel(
        gg_ref, proj_ref, taps_ref, kern_ref, fwd_ref, inv_ref, filt_ref, spec_ref,
        gproj_ref, gkern_ref, gtaps_ref, grad_spec,
    )
    _, vocab, _ = table_ref.shape
    seq = filt_ref.shape[0]
    entry = lax.broadcasted_iota(jnp.int32, (vocab, seq), 0)
    chosen = (entry == tokens_ref[...]).astype(F32).astype(BF16)
    for m in range(3):
        table_ref[m] = (dot(chosen, gproj_ref[0, m]) * scale_ref[...]).astype(BF16)


def forward_kernel(proj_ref, taps_ref, kern_ref, fwd_ref, inv_ref, gated_ref, filt_ref, spec_ref):
    tap_count, chans = kern_ref.shape
    blocks = filt_ref.shape[0] // tap_count
    row = lax.broadcasted_iota(jnp.int32, (tap_count, chans), 0)
    sign = jnp.where(row % 2 == 0, 1.0, -1.0)
    kr, ki, kn = kernel_spectrum(fwd_ref, kern_ref, row)
    zero = jnp.zeros((tap_count, chans), F32)
    before = [zero] * 3
    last_r, last_i = zero, zero
    for b in range(blocks):
        here = pl.ds(b * tap_count, tap_count)
        streams = []
        for m in range(3):
            current = proj_block(proj_ref, m, b, tap_count)
            streams.append(short_filter(taps_ref, m, current, before[m], row))
            before[m] = current
        part = dot(fwd_ref[...], (streams[1] * streams[2]).astype(BF16))
        pr, pi = part[:tap_count], part[tap_count:]
        wr = last_r + sign * pr
        wi = last_i + sign * pi
        last_r, last_i = pr, pi
        spec_ref[b, :tap_count, :] = wr.astype(BF16)
        spec_ref[b, tap_count:, :] = wi.astype(BF16)
        mixed = jnp.concatenate([wr * kr - wi * ki, wr * ki + wi * kn], axis=0)
        filtered = dot(inv_ref[...], mixed.astype(BF16))
        filt_ref[here, :] = filtered.astype(BF16)
        gated_ref[here, :] = (streams[0] * filtered).astype(BF16)


def backward_kernel(
    gg_ref, proj_ref, taps_ref, kern_ref, fwd_ref, inv_ref, filt_ref, spec_ref,
    gproj_ref, gkern_ref, gtaps_ref, grad_spec,
):
    tap_count, chans = kern_ref.shape
    blocks = filt_ref.shape[0] // tap_count
    row = lax.broadcasted_iota(jnp.int32, (tap_count, chans), 0)
    sign = jnp.where(row % 2 == 0, 1.0, -1.0)
    kr, ki, kn = kernel_spectrum(fwd_ref, kern_ref, row)
    zero = jnp.zeros((tap_count, chans), F32)
    sum_r, sum_i = zero, zero
    last = zero
    for b in range(blocks):
        here = pl.ds(b * tap_count, tap_count)
        current = proj_block(proj_ref, 0, b, tap_count)
        query = short_filter(taps_ref, 0, current, last, row)
        last = current
        part = dot(fwd_ref[...], (gg_ref[here, :].astype(F32) * query).astype(BF16))
        grad_spec[b] = part
        gr, gi = sign * part[:tap_count], sign * part[tap_count:]
        wr = spec_ref[b, :tap_count, :].astype(F32)
        wi = spec_ref[b, tap_count:, :].astype(F32)
        rr, ii = wr * gr, wi * gi
        sum_r = sum_r + jnp.where(row == 0, rr, rr + ii)
        sum_i = sum_i + jnp.where(row == 0, ii, wr * gi - wi * gr)
    gkern_ref[...] = exact(
        inv_ref[...].astype(F32), jnp.concatenate([sum_r, sum_i], axis=0)
    )
    after = [zero] * 3
    next_r, next_i = zero, zero
    sums = [jnp.zeros((1, chans), F32) for _ in range(9)]
    for b in reversed(range(blocks)):
        chunk, start = divmod(b * tap_count, proj_ref.shape[2])
        here = pl.ds(b * tap_count, tap_count)
        gr, gi = grad_spec[b, :tap_count, :], grad_spec[b, tap_count:, :]
        vr, vi = gr + sign * next_r, gi + sign * next_i
        next_r, next_i = gr, gi
        mixed = jnp.concatenate([vr * kr + vi * ki, vi * kn - vr * ki], axis=0)
        grad_prod = dot(inv_ref[...], mixed.astype(BF16))
        shifts, shorts = [], []
        for m in range(3):
            current = proj_block(proj_ref, m, b, tap_count)
            before = proj_block(proj_ref, m, b - 1, tap_count) if b else zero
            shifts.append([current, later(current, before, 1, row), later(current, before, 2, row)])
            if m:
                shorts.append(sum(taps_ref[3 * j + m : 3 * j + m + 1, :] * shifts[m][j] for j in range(3)))
        grads = [
            gg_ref[here, :].astype(F32) * filt_ref[here, :].astype(F32),
            grad_prod * shorts[1],
            grad_prod * shorts[0],
        ]
        for m in range(3):
            grad = grads[m]
            out = (
                taps_ref[m : m + 1, :] * grad
                + taps_ref[3 + m : 4 + m, :] * sooner(grad, after[m], 1, row)
                + taps_ref[6 + m : 7 + m, :] * sooner(grad, after[m], 2, row)
            )
            after[m] = grad
            gproj_ref[chunk, m, start : start + tap_count, :] = out.astype(BF16)
            for j in range(3):
                sums[3 * j + m] = sums[3 * j + m] + jnp.sum(
                    grad * shifts[m][j], axis=0, keepdims=True
                )
    for index in range(9):
        gtaps_ref[index : index + 1, :] = sums[index]


PARAMS = pltpu.CompilerParams(vmem_limit_bytes=56 * 1024 * 1024)


def conv_forward(proj, taps, kern, matrices, tokens=None):
    tap_count, chans = kern.shape
    seq = proj.shape[0] * proj.shape[2] if tokens is None else tokens.shape[0]
    results = [
        jax.ShapeDtypeStruct((seq, chans), BF16),
        jax.ShapeDtypeStruct((seq, chans), BF16),
        jax.ShapeDtypeStruct((seq // tap_count, 2 * tap_count, chans), BF16),
    ]
    operands = (proj, taps, kern, matrices[0], matrices[2])
    if tokens is not None:
        results.append(jax.ShapeDtypeStruct((1, 3, seq, chans), BF16))
        operands = (tokens[:, None], *operands)
    return pl.pallas_call(
        forward_kernel if tokens is None else lookup_kernel,
        out_shape=results,
        compiler_params=PARAMS,
        name="conv_forward",
    )(*operands)


def conv_backward(gg, proj, taps, kern, matrices, saved, tokens=None, scale=None):
    tap_count, chans = kern.shape
    seq = gg.shape[0]
    scratch = [pltpu.VMEM((seq // tap_count, 2 * tap_count, chans), F32)]
    operands = (gg, proj, taps, kern, matrices[0], matrices[1], *saved)
    first = jax.ShapeDtypeStruct(proj.shape, BF16)
    if tokens is not None:
        first = jax.ShapeDtypeStruct((3, scale.shape[0], chans), BF16)
        scratch.append(pltpu.VMEM(proj.shape, BF16))
        operands = (tokens[None, :], scale, *operands)
    return pl.pallas_call(
        backward_kernel if tokens is None else collect_kernel,
        out_shape=(
            first,
            jax.ShapeDtypeStruct(kern.shape, F32),
            jax.ShapeDtypeStruct((9, chans), F32),
        ),
        scratch_shapes=scratch,
        compiler_params=PARAMS,
        name="conv_backward",
    )(*operands)


def table_projection(table, weights, ctx, order, kind):
    vocab, feats = table.shape
    sub = weights.shape[2] // lax.axis_size("ctx")
    if sub % 128:
        columns = jnp.stack(
            [lax.dynamic_slice_in_dim(weights, (ctx ^ r) * sub, sub, 2) for r in order]
        )
        return jnp.einsum("vd,rmdc->rmvc", table, columns, preferred_element_type=F32).astype(kind)

    def kernel(where_ref, table_ref, weights_ref, out_ref):
        for m in range(3):
            out_ref[0, m] = dot(table_ref[...], weights_ref[m]).astype(kind)

    return pl.pallas_call(
        kernel,
        grid_spec=pltpu.PrefetchScalarGridSpec(
            num_scalar_prefetch=1,
            grid=(len(order),),
            in_specs=[
                pl.BlockSpec((vocab, feats), lambda r, where: (0, 0)),
                pl.BlockSpec((3, feats, sub), lambda r, where: (0, 0, where[r])),
            ],
            out_specs=pl.BlockSpec((1, 3, vocab, sub), lambda r, where: (r, 0, 0, 0)),
        ),
        out_shape=jax.ShapeDtypeStruct((len(order), 3, vocab, sub), kind),
        compiler_params=PARAMS,
        name="table_projection",
    )(jnp.stack([ctx ^ r for r in order]), table, weights)


def input_projection(rows_in, pieces, ctx):
    rows, full_width = rows_in.shape
    feats, chans = pieces[0].shape[1:]
    count = len(pieces)
    sub = chans // count

    def kernel(ctx_ref, rows_ref, *refs):
        weights, (normed_ref, proj_ref, scale_ref) = refs[:count], refs[count:]

        @pl.when(pl.program_id(0) == 0)
        def _():
            total = jnp.zeros((rows, 1), F32)
            for q in range(count):
                part = rows_ref[:, q * feats : (q + 1) * feats].astype(F32)
                total = total + jnp.sum(part * part, axis=1, keepdims=True)
            scale_ref[...] = lax.rsqrt(total / full_width + EPSILON)
            for q in range(count):
                part = rows_ref[:, q * feats : (q + 1) * feats].astype(F32)
                normed_ref[q] = (part * scale_ref[...]).astype(BF16)

        total = jnp.zeros((rows, chans), F32)
        for r in range(count):
            start = pl.multiple_of((ctx_ref[0] ^ r) * feats, feats)
            total = total + dot(rows_ref[:, pl.ds(start, feats)], weights[r][0])
        total = (total * scale_ref[...]).astype(BF16)
        for q in range(count):
            proj_ref[q, 0] = total[:, q * sub : (q + 1) * sub]

    return pl.pallas_call(
        kernel,
        grid_spec=pltpu.PrefetchScalarGridSpec(
            num_scalar_prefetch=1,
            grid=(3,),
            in_specs=[pl.BlockSpec((rows, full_width), lambda m, ctx: (0, 0))]
            + [pl.BlockSpec((1, feats, chans), lambda m, ctx: (m, 0, 0))] * count,
            out_specs=[
                pl.BlockSpec((count, rows, feats), lambda m, ctx: (0, 0, 0)),
                pl.BlockSpec((count, 1, rows, sub), lambda m, ctx: (0, m, 0, 0)),
                pl.BlockSpec((rows, 1), lambda m, ctx: (0, 0)),
            ],
        ),
        out_shape=(
            jax.ShapeDtypeStruct((count, rows, feats), BF16),
            jax.ShapeDtypeStruct((count, 3, rows, sub), BF16),
            jax.ShapeDtypeStruct((rows, 1), F32),
        ),
        compiler_params=PARAMS,
        name="input_projection",
    )(ctx[None], rows_in, *pieces)


def input_gradient(gproj, pieces, rows_in, scale, ctx):
    rows, full_width = rows_in.shape
    feats, chans = pieces[0].shape[1:]
    count = len(pieces)
    sub = chans // count
    tile = min(256, feats)
    steps = feats // tile

    def kernel(ctx_ref, gproj_ref, rows_ref, scale_ref, *refs):
        weights, (out_ref, flat, grads) = refs[:count], refs[count:]
        step = pl.program_id(0)

        @pl.when(step == 0)
        def _():
            for m in range(3):
                for q in range(count):
                    flat[m, :, q * sub : (q + 1) * sub] = gproj_ref[q, m]

        columns = pl.ds(pl.multiple_of(step * tile, tile), tile)
        for r in range(count):
            total = dot_t(flat[0], weights[r][0])
            for m in (1, 2):
                total = total + dot_t(flat[m], weights[r][m])
            grads[ctx_ref[0] ^ r, :, columns] = total * scale_ref[...]

        @pl.when(step == steps - 1)
        def _():
            stat = jnp.zeros((rows, 1), F32)
            for q in range(count):
                part = rows_ref[:, q * feats : (q + 1) * feats].astype(F32)
                stat = stat + jnp.sum(part * grads[q], axis=1, keepdims=True)
            stat = stat * scale_ref[...] * scale_ref[...] / full_width
            for q in range(count):
                part = rows_ref[:, q * feats : (q + 1) * feats].astype(F32)
                out_ref[q] = (grads[q] - part * stat).astype(BF16)

    return pl.pallas_call(
        kernel,
        grid_spec=pltpu.PrefetchScalarGridSpec(
            num_scalar_prefetch=1,
            grid=(steps,),
            in_specs=[
                pl.BlockSpec(gproj.shape, lambda t, ctx: (0, 0, 0, 0)),
                pl.BlockSpec((rows, full_width), lambda t, ctx: (0, 0)),
                pl.BlockSpec((rows, 1), lambda t, ctx: (0, 0)),
            ]
            + [pl.BlockSpec((3, tile, chans), lambda t, ctx: (0, t, 0))] * count,
            out_specs=pl.BlockSpec((count, rows, feats), lambda t, ctx: (0, 0, 0)),
            scratch_shapes=[
                pltpu.VMEM((3, rows, chans), BF16),
                pltpu.VMEM((count, rows, feats), F32),
            ],
        ),
        out_shape=jax.ShapeDtypeStruct((count, rows, feats), BF16),
        compiler_params=PARAMS,
        name="input_gradient",
    )(ctx[None], gproj, rows_in, scale, *pieces)


def grad_in_kernel(left, pieces, ctx):
    feats, depth = left.shape
    count, sub = len(pieces), pieces[0].shape[2]
    if sub % 128:
        columns = jnp.concatenate([pick(jnp.stack(pieces), ctx ^ q) for q in range(count)], axis=2)
        return jnp.einsum("dk,mkc->mdc", left, columns, preferred_element_type=F32)

    tile = min(256, feats)

    def kernel(ctx_ref, left_ref, *refs):
        out_ref = refs[count]
        for r in range(count):
            columns = pl.ds(pl.multiple_of((ctx_ref[0] ^ r) * sub, sub), sub)
            for m in range(3):
                out_ref[m, :, columns] = dot(left_ref[...], refs[r][m])

    return pl.pallas_call(
        kernel,
        grid_spec=pltpu.PrefetchScalarGridSpec(
            num_scalar_prefetch=1,
            grid=(feats // tile,),
            in_specs=[pl.BlockSpec((tile, depth), lambda t, ctx: (t, 0))]
            + [pl.BlockSpec((3, depth, sub), lambda t, ctx: (0, 0, 0))] * count,
            out_specs=pl.BlockSpec((3, tile, sub * count), lambda t, ctx: (0, t, 0)),
        ),
        out_shape=jax.ShapeDtypeStruct((3, feats, sub * count), F32),
        compiler_params=PARAMS,
        name="grad_project_in",
    )(ctx[None], left, *pieces)


def grad_out_kernel(pieces, right, ctx):
    depth, feats = right.shape
    count, sub = len(pieces), pieces[0].shape[0]

    def kernel(where_ref, right_ref, *refs):
        out_ref = refs[count]
        for r in range(count):

            @pl.when(pl.program_id(0) == r)
            def _():
                out_ref[...] = dot(refs[r][...], right_ref[...])

    return pl.pallas_call(
        kernel,
        grid_spec=pltpu.PrefetchScalarGridSpec(
            num_scalar_prefetch=1,
            grid=(count,),
            in_specs=[pl.BlockSpec((depth, feats), lambda r, where: (0, 0))]
            + [pl.BlockSpec((sub, depth), lambda r, where: (0, 0))] * count,
            out_specs=pl.BlockSpec((sub, feats), lambda r, where: (where[r], 0)),
        ),
        out_shape=jax.ShapeDtypeStruct((sub * count, feats), F32),
        compiler_params=PARAMS,
        name="grad_project_out",
    )(jnp.stack([ctx ^ r for r in range(count)]), right, *pieces)


def together(*values):
    return lax.optimization_barrier(values)


def output_projection(gated, weights, chunks):
    count, rows, sub = gated.shape
    chans, full_width = weights.shape
    width = full_width // chunks

    def kernel(gated_ref, weights_ref, out_ref, flat):
        @pl.when(pl.program_id(0) == 0)
        def _():
            for q in range(count):
                flat[:, q * sub : (q + 1) * sub] = gated_ref[q]

        out_ref[0] = dot(flat[...], weights_ref[...]).astype(BF16)

    return pl.pallas_call(
        kernel,
        grid=(chunks,),
        in_specs=[
            pl.BlockSpec(gated.shape, lambda q: (0, 0, 0)),
            pl.BlockSpec((chans, width), lambda q: (0, q)),
        ],
        out_specs=pl.BlockSpec((1, rows, width), lambda q: (q, 0, 0)),
        out_shape=jax.ShapeDtypeStruct((chunks, rows, width), BF16),
        scratch_shapes=[pltpu.VMEM((rows, chans), BF16)],
        compiler_params=PARAMS,
        name="output_projection",
    )(gated, weights)


def ctx_swap(value):
    return lax.all_to_all(value, "ctx", split_axis=0, concat_axis=0, tiled=True)


def local(
    token_ids, embedding, project_in, short_taps, filter_taps, decay_rates, project_out, cotangent
):
    n_ctx, n_dp = lax.axis_size("ctx"), lax.axis_size("dp")
    sec, dp, ctx = (lax.axis_index(axis) for axis in ("section", "dp", "ctx"))
    first = sec == 0
    rows, vocab = token_ids.shape[0], embedding.shape[0]
    seq = rows * n_ctx
    weights_in = jnp.transpose(project_in[0], (1, 0, 2))
    weights_out = project_out[0]
    feats, chans = weights_out.shape[1], weights_out.shape[0]
    full_width = feats * n_ctx
    sub = chans // n_ctx

    if n_ctx == n_dp:
        half = vocab // 2
        mine = lax.dynamic_slice_in_dim(embedding, sec * half, half, 0)
        came = []
        for i in range(1, n_dp):
            shifts = (i, i % (n_dp - 1) + 1)
            came.append(
                send(
                    mine,
                    ("section", "dp", "ctx"),
                    lambda s, z, k: (0, (z + shifts[s]) % n_dp, k) if z == k else None,
                )
            )
        offset = (dp - ctx) % n_dp
        low, high = embedding[:half], embedding[half:]
        for i in range(1, n_dp):
            low = jnp.where(offset == i, came[i - 1], low)
            high = jnp.where(offset == i % (n_dp - 1) + 1, came[i - 1], high)
        table = jnp.concatenate([low, high], axis=0)
    else:
        table = lax.dynamic_slice_in_dim(
            lax.all_gather(embedding, "dp", axis=1, tiled=True), ctx * feats, feats, 1
        )
    table_float = embedding.astype(F32)
    shared = jnp.concatenate(
        [jnp.sum(table_float * table_float, axis=1), token_ids.astype(F32)]
    )
    shared = lax.all_gather(shared, ("dp", "ctx"), axis=0)
    table, shared = together(table, shared)
    shared = shared.reshape(n_dp, n_ctx, vocab + rows)
    table_inv = lax.rsqrt(
        jnp.sum(shared[:, 0, :vocab], axis=0)[:, None] / full_width + EPSILON
    )
    tokens = shared[0, :, vocab:].reshape(seq).astype(jnp.int32)

    def own(value):
        return lax.dynamic_slice_in_dim(value, ctx * sub, sub, value.ndim - 1)

    taps = own(short_taps[0]).reshape(9, sub)
    filters = own(filter_taps[0])
    tap_count = filters.shape[0]
    positions = jnp.arange(tap_count).astype(F32)[:, None]
    damping = jnp.exp(-own(decay_rates) * positions / tap_count)
    kern = filters * damping
    matrices = spectra(tap_count)

    vocabulary = jnp.arange(vocab, dtype=jnp.int32)[None, :]
    first_input = dot((token_ids[:, None] == vocabulary).astype(BF16), embedding)

    out_full = lax.all_gather(weights_out, "ctx", axis=1, tiled=True)
    in_far = {0: weights_in}
    bit = n_ctx // 2
    while bit > 1:
        for r in list(in_far):
            in_far[r | bit] = ctx_xor(in_far[r], bit, (1,))
        bit //= 2

    order = scatter_order(n_ctx)
    kept = order[: n_ctx // 2]
    sent = table_projection(table, weights_in, ctx, [r | 1 for r in kept], BF16)
    arrived = ctx_xor(sent, 1, (0,))
    partial = table_projection(table, weights_in, ctx, kept, F32) + arrived.astype(F32)
    bit = 2
    while bit < n_ctx:
        stays, gone = jnp.split(partial, 2, axis=0)
        partial = stays + ctx_xor(gone.astype(BF16), bit, (0,)).astype(F32)
        bit *= 2
    table_proj = (partial[0] * table_inv).astype(BF16)
    gated_0, *saved_0, proj_0 = conv_forward(table_proj, taps, kern, matrices, tokens)
    gated_rows = ctx_swap(gated_0.reshape(n_ctx, rows, sub))
    middle = cross_sum(output_projection(gated_rows, out_full, n_dp), 0)
    middle = (first_input + middle).astype(BF16)

    held = sorted(in_far)[1:]
    middle, *late = together(middle, *[in_far[r] for r in held])
    in_far.update(zip(held, late))
    in_pieces = []
    for r in sorted(in_far):
        in_pieces += [in_far[r], ctx_xor(in_far[r], 1, (1,))]
    middle_all = jnp.concatenate(in_order(dp_gather(middle, 1, 2), dp), axis=1)
    normed, proj_rows, scale = input_projection(middle_all, in_pieces, ctx)
    proj_1 = ctx_swap(proj_rows)
    gated_1, *saved_1 = conv_forward(proj_1, taps, kern, matrices)

    def gated_grad(rows_all):
        total = dot_t(rows_all, out_full).astype(BF16)
        split = jnp.transpose(total.reshape(rows, n_ctx, sub), (1, 0, 2))
        return ctx_swap(split).reshape(seq, sub)

    cot_parts = in_order(dp_gather(cotangent, 1, 1), dp)
    cot_all = jnp.concatenate(cot_parts, axis=1)
    gproj_1, gkern_1, gtaps_1 = conv_backward(
        gated_grad(cot_all), proj_1, taps, kern, matrices, saved_1
    )
    gproj_rows = ctx_swap(gproj_1)
    shares = input_gradient(gproj_rows, in_pieces, middle_all, scale, ctx)
    shares, normed, gproj_1, gated_1 = together(shares, normed, gproj_1, gated_1)
    grad_middle = (cotangent.astype(F32) + cross_sum(shares, 1)).astype(BF16)

    swapped = [pick(normed, ctx)]
    for r in range(1, n_ctx):
        swapped.append(ctx_xor(pick(normed, ctx ^ r), r, (1,)))
    swapped = jnp.stack(swapped)
    normed_cols = jnp.concatenate([pick(swapped, ctx ^ q).T for q in range(n_ctx)], axis=1)
    gproj_all = ctx_gather(gproj_1.transpose(1, 0, 2, 3).reshape(3, seq, sub), (1,))
    gated_all = ctx_gather(jnp.where(first, gated_0, gated_1).T, (0, 1))

    back_stack = dp_gather(grad_middle, 0, 2)
    back_stack, normed_cols, *rest = together(back_stack, normed_cols, *gproj_all, *gated_all)
    gproj_all, gated_all = rest[:n_ctx], rest[n_ctx:]
    back_parts = in_order(back_stack, dp)
    table_grad, gkern_0, gtaps_0 = conv_backward(
        gated_grad(jnp.concatenate(back_parts, axis=1)),
        proj_0, taps, kern, matrices, saved_0, tokens, table_inv,
    )

    if n_ctx == n_dp:
        grads = jnp.stack([jnp.where(first, a, b) for a, b in zip(back_parts, cot_parts)])
    else:
        grads = jnp.where(first, jnp.concatenate(back_parts, axis=1), cot_all)
        grads = jnp.transpose(grads.reshape(rows, n_ctx, feats), (1, 0, 2))
    grad_cols = ctx_swap(grads).reshape(seq, feats)
    grad_out = grad_out_kernel(gated_all, grad_cols, ctx)
    table_all = {0: table_grad}
    bit = n_ctx // 2
    while bit > 1:
        for r in list(table_all):
            table_all[r | bit] = ctx_xor(table_all[r], bit, (0,))
        bit //= 2
    held = sorted(table_all)[1:]
    grad_out, *late = together(grad_out, *[table_all[r] for r in held])
    table_all.update(zip(held, late))
    table_pieces = []
    for r in sorted(table_all):
        table_pieces += [table_all[r], ctx_xor(table_all[r], 1, (0,))]
    grad_in = lax.cond(
        first,
        lambda: grad_in_kernel(table.T, table_pieces, ctx),
        lambda: grad_in_kernel(normed_cols, gproj_all, ctx),
    )

    gkern = jnp.where(first, gkern_0, gkern_1)
    gtaps = jnp.where(first, gtaps_0, gtaps_1)
    gdecay = -jnp.sum(gkern * kern * positions, axis=0, keepdims=True) / tap_count
    small = jnp.concatenate([gkern * damping, gdecay, gtaps], axis=0)
    small = jnp.stack(ctx_gather(small, (0, 1)))
    small = jnp.concatenate([pick(small, ctx ^ q) for q in range(n_ctx)], axis=1)
    return (
        jnp.transpose(grad_in, (1, 0, 2))[None],
        grad_out[None],
        small[:tap_count][None],
        small[tap_count][None],
        small[tap_count + 1 :].reshape(1, 3, 3, chans),
    )


def solution(mesh):
    return jax.shard_map(
        local,
        mesh=mesh,
        in_specs=(
            P("ctx"),
            P(None, "dp"),
            P("section", "ctx", None, "dp"),
            P("section", None, None, "dp"),
            P("section", None, "dp"),
            P("section", "dp"),
            P("section", "dp", "ctx"),
            P("ctx", "dp"),
        ),
        out_specs=(
            P("section", "ctx", None, "dp"),
            P("section", "dp", "ctx"),
            P("section", None, "dp"),
            P("section", "dp"),
            P("section", None, None, "dp"),
        ),
        check_vma=False,
    )
```

time: 915 us -> 700 us (0.77)
  waiting for transfers between devices: 475 us -> 208 us
  starting transfers between devices: 34.6 us -> 246 us
  matrix products: 147 us -> 8.66 us
  local copies, waits for them, and re-layouts: 120 us -> 29.4 us
  Pallas kernels: 0 us -> 89.6 us
  other arithmetic: 71.7 us -> 33.4 us
  blocking collectives: 43 us -> 61.4 us
    all_gather x8 -> x1, waiting for transfers between devices: 290 us -> 0.01 us  [local(): out_full = lax.all_gather(weights_out, 'ctx', axis=1, tiled=True)]
    ppermute x10 -> x46, starting transfers between devices: 25.3 us -> 221 us  [send(): return lax.ppermute(value, axes, pairs)]
    ppermute x10 -> x46, waiting for transfers between devices: 42.1 us -> 181 us  [send(): return lax.ppermute(value, axes, pairs)]
    pallas_call x0 -> x11, Pallas kernels: none -> 89.6 us  [the longest x2 15.9 us: conv_backward(): pl.pallas_call(backward_kernel if tokens is None else collect_kernel, out...]
    psum x2 -> x0, waiting for transfers between devices: 77.3 us -> none  [the longest x1 77.2 us: backward(): lax.psum(partials.astype(jnp.bfloat16), 'dp').astype(jnp.float32)]
    dot_general x9 -> x3, matrix products: 82 us -> 8.66 us  [the longest x2 8.1 us: dot_t(): lax.dot_general(left, right, (((1,), (1,)), ((), ())), preferred_element_...]
    conv_general_dilated x6 -> x0, matrix products: 65 us -> none  [correlate(): lax.conv_general_dilated(signal[None], kernel[:, None, :], (1,), 'VALID',...]
    reduce_scatter x1 -> x0, waiting for transfers between devices: 45.5 us -> none  [forward(): lax.psum_scatter(partials.astype(jnp.bfloat16), 'dp', scatter_dimension=1...]
  transfers between devices with their start and end apart: 23 -> 52, of which waited for: 15 -> 17; matrix products, arithmetic and copies ran while one was open for 23% -> 8% of each run, Pallas kernels for 0% -> 8%
where the time goes in v1:
time: 700 us; the launch traced here: 691 us
  starting transfers between devices  246 us (35%)
  waiting for transfers between devices  208 us (30%)
  Pallas kernels  89.6 us (13%)
  blocking collectives  61.4 us (9%)
  other arithmetic  33.4 us (5%)
  local copies, waits for them, and re-layouts  29.4 us (4%)
  between operations  15.2 us (2%)
  matrix products  8.66 us (1%)
    ppermute x46, starting transfers between devices, send(): return lax.ppermute(value, axes, pairs)  221 us
    ppermute x46, waiting for transfers between devices, send(): return lax.ppermute(value, axes, pairs)  181 us
    all_gather x1, blocking collectives, local(): shared = lax.all_gather(shared, ('dp', 'ctx'), axis=0)  37.1 us
    all_to_all x5, waiting for transfers between devices, ctx_swap(): return lax.all_to_all(value, 'ctx', split_axis=0, concat_axis=0, tiled=True)  26.2 us
    all_to_all x5, starting transfers between devices, ctx_swap(): return lax.all_to_all(value, 'ctx', split_axis=0, concat_axis=0, tiled=True)  24.8 us
    all_to_all x1, blocking collectives, ctx_swap(): return lax.all_to_all(value, 'ctx', split_axis=0, concat_axis=0, tiled=True)  24.3 us
    pallas_call x2, Pallas kernels, conv_backward(): pl.pallas_call(backward_kernel if tokens is None else collect_kernel, out...  15.9 us
    pallas_call x1, Pallas kernels, input_projection(): pl.pallas_call(kernel, grid_spec=pltpu.PrefetchScalarGridSpec(num_scalar_...  15.5 us
  transfers between devices with their start and end apart: 52, of which 17 were waited for; matrix products, arithmetic and copies ran while one was open for 8% of the time, Pallas kernels for 8%

profile of v1, /device:TPU:1, one launch (start us, length us, event | category | flops | bytes accessed | tf_op | source)
XLA Modules:
  0.0 691.0 jit_solution(15709766756962568131)
XLA Ops:
  14.9 37.1 %all-gather.2 = f32[16,1,768]{2,1,0:T(1,128)S(1)} all-gather(f32[1,1,768]{2,1,0:T(1,128)S(1)} %reshape.123), channel_id=3, replica_groups=mesh['section'=2,'dp'=4,'ctx'=4] {'dp','ctx'}, dimensions={0}, use_global_device_ids=true | all-gather | bytes 52224 | tf_op jit(solution)/shard_map/all_gather | solution.py:601
  76.1 16.1 %collective-permute-done.7 = bf16[1,3,512,256]{3,2,1,0:T(8,128)(2,1)} collective-permute-done((bf16[1,3,512,256]{3,2,1,0:T(8,128)(2,1)S(1)}, bf16[1,3,512,256]{3,2,1,0:T(8,128)(2,1)}, u32[]{:S(2)}, u32[]{:S(2)}) %collective-permute-start.7) | collective-permute-done | bytes 786464 | tf_op jit(solution)/shard_map/ppermute | solution.py:39
  94.9 5.6 conv_forward.2
  105.1 8.0 %all-to-all-done.1.gated_ref = bf16[4,256,256]{2,1,0:T(8,128)(2,1)S(1)} async-done(((bf16[4,256,256]{2,1,0:T(8,128)(2,1)}), bf16[4,256,256]{2,1,0:T(8,128)(2,1)S(1)}, u32[]{:S(2)}, u32[]{:S(2)}) %all-to-all-start.1) | async-done | bytes 524320 | tf_op jit(solution)/shard_map/all_to_all | solution.py:557
  113.9 6.7 output_projection.1
  122.3 140.3 %collective-permute-start.11 = (bf16[256,1024]{1,0:T(8,128)(2,1)S(1)}, bf16[256,1024]{1,0:T(8,128)(2,1)S(1)}, u32[]{:S(2)}, u32[]{:S(2)}) collective-permute-start(bf16[256,1024]{1,0:T(8,128)(2,1)S(1)} %get-tuple-element.173), channel_id=1, source_target_pairs={{0,28},{4,16},{8,20},{12,24},{1,29},{5,17},{9,21},{13,25},{2,30},{... | collective-permute-start | bytes 1572872 | tf_op jit(solution)/shard_map/ppermute | solution.py:39
  276.4 7.9 %collective-permute-done.10 = bf16[256,1024]{1,0:T(8,128)(2,1)S(1)} collective-permute-done((bf16[256,1024]{1,0:T(8,128)(2,1)S(1)}, bf16[256,1024]{1,0:T(8,128)(2,1)S(1)}, u32[]{:S(2)}, u32[]{:S(2)}) %collective-permute-start.10) | collective-permute-done | bytes 524320 | tf_op jit(solution)/shard_map/ppermute | solution.py:39
  284.3 11.2 %collective-permute-done.9 = bf16[256,1024]{1,0:T(8,128)(2,1)S(1)} collective-permute-done((bf16[256,1024]{1,0:T(8,128)(2,1)S(1)}, bf16[256,1024]{1,0:T(8,128)(2,1)S(1)}, u32[]{:S(2)}, u32[]{:S(2)}) %collective-permute-start.9) | collective-permute-done | bytes 524320 | tf_op jit(solution)/shard_map/ppermute | solution.py:39
  295.6 15.1 %collective-permute-done.8 = bf16[256,1024]{1,0:T(8,128)(2,1)S(1)} collective-permute-done((bf16[256,1024]{1,0:T(8,128)(2,1)S(1)}, bf16[256,1024]{1,0:T(8,128)(2,1)S(1)}, u32[]{:S(2)}, u32[]{:S(2)}) %collective-permute-start.8) | collective-permute-done | bytes 524320 | tf_op jit(solution)/shard_map/ppermute | solution.py:39
  328.9 15.5 %input_projection.1 = (bf16[4,256,1024]{2,1,0:T(8,128)(2,1)}, bf16[4,3,256,256]{3,2,1,0:T(8,128)(2,1)}, f32[256,1]{1,0:T(8,128)}) custom-call(s32[1]{0:T(128)} %bitcast.3.ctx_ref, bf16[256,4096]{1,0:T(8,128)(2,1)} %pad_maximum_fusion.2.rows_ref, bf16[3,1024,1024]{2,1,0:T(8,128)(2,1)} %bitcast.17.weights_ref.refs_0_, ...), custom_call_target="tpu_custom_call" | custom-call | tf_op jit(solution)/shard_map/input_projection/pallas_call | solution.py:384
  352.0 5.7 fusion.22
  358.6 10.0 %all-to-all-done.2.proj_ref = bf16[4,3,256,256]{3,2,1,0:T(8,128)(2,1)} async-done(((bf16[4,3,256,256]{3,2,1,0:T(8,128)(2,1)}), bf16[4,3,256,256]{3,2,1,0:T(8,128)(2,1)}, u32[]{:S(2)}, u32[]{:S(2)}) %all-to-all-start.2) | async-done | bytes 1572896 | tf_op jit(solution)/shard_map/all_to_all | solution.py:557
  368.6 5.4 all-to-all-start
  382.0 7.5 %conv_backward.2 = (bf16[4,3,256,256]{3,2,1,0:T(8,128)(2,1)}, f32[128,256]{1,0:T(8,128)}, f32[9,256]{1,0:T(8,128)}) custom-call(bf16[1024,256]{1,0:T(8,128)(2,1)} %bitcast.14.gg_ref, bf16[4,3,256,256]{3,2,1,0:T(8,128)(2,1)} %all-to-all-done.2.proj_ref, f32[9,256]{1,0:T(8,128)} %reshape.114.taps_ref, f32[128,256]{1,0:T(8,128)} %bitcast_multiply_fusion.kern_ref, ...), custom_call_target="tpu_custom_call" | custom-call | tf_op jit(solution)/shard_map/conv_backward/pallas_call | solution.py:313
  389.5 24.3 %all_to_all.30.gproj_ref = bf16[4,3,256,256]{3,2,1,0:T(8,128)(2,1)} all-to-all(bf16[4,3,256,256]{3,2,1,0:T(8,128)(2,1)} %get-tuple-element.94), channel_id=1, replica_groups=mesh['section'=2,'dp'=4,'ctx'=4] {'ctx'}, dimensions={0} | all-to-all | bytes 3145728 | tf_op jit(solution)/shard_map/all_to_all | solution.py:557
  413.9 15.3 %input_gradient.1 = bf16[4,256,1024]{2,1,0:T(8,128)(2,1)} custom-call(s32[1]{0:T(128)} %bitcast.3.ctx_ref, bf16[4,3,256,256]{3,2,1,0:T(8,128)(2,1)} %all_to_all.30.gproj_ref, bf16[256,4096]{1,0:T(8,128)(2,1)} %pad_maximum_fusion.2.rows_ref, f32[256,1]{1,0:T(8,128)} %get-tuple-element.89.scale_ref, bf16[3,1024,1024]{2,1,0:T(8,128)(2,1)} %bitcast.17.weights_ref.refs_0_, ...), custom_call_target="tpu_custom_call" | custom-call | tf_op jit(solution)/shard_map/input_gradient/pallas_call | solution.py:443
  441.6 58.5 %collective-permute-done.24 = bf16[256,1024]{1,0:T(8,128)(2,1)} collective-permute-done((bf16[256,1024]{1,0:T(8,128)(2,1)}, bf16[256,1024]{1,0:T(8,128)(2,1)}, u32[]{:S(2)}, u32[]{:S(2)}) %collective-permute-start.24) | collective-permute-done | bytes 524320 | tf_op jit(solution)/shard_map/ppermute | solution.py:39
  501.6 30.7 %collective-permute-done.23 = bf16[256,1024]{1,0:T(8,128)(2,1)} collective-permute-done((bf16[256,1024]{1,0:T(8,128)(2,1)}, bf16[256,1024]{1,0:T(8,128)(2,1)}, u32[]{:S(2)}, u32[]{:S(2)}) %collective-permute-start.23) | collective-permute-done | bytes 524320 | tf_op jit(solution)/shard_map/ppermute | solution.py:39
  589.6 5.5 all-to-all-start.4
  609.2 8.4 %conv_backward.3 = (bf16[3,512,256]{2,1,0:T(8,128)(2,1)}, f32[128,256]{1,0:T(8,128)}, f32[9,256]{1,0:T(8,128)}) custom-call(s32[1,1024]{1,0:T(1,128)} %bitcast.184, f32[512,1]{1,0:T(8,128)} %copy.36.scale_ref, bf16[1024,256]{1,0:T(8,128)(2,1)} %bitcast.172, bf16[1,3,1024,256]{3,2,1,0:T(8,128)(2,1)} %get-tuple-element.102.proj_ref, ...), custom_call_target="tpu_custom_call" | custom-call | tf_op jit(solution)/shard_map/conv_backward/pallas_call | solution.py:313
  624.1 29.2 %collective-permute-done.44 = f32[138,256]{1,0:T(8,128)} collective-permute-done((f32[138,256]{1,0:T(8,128)}, f32[138,256]{1,0:T(8,128)}, u32[]{:S(2)}, u32[]{:S(2)}) %collective-permute-start.44) | collective-permute-done | bytes 141344 | tf_op jit(solution)/shard_map/ppermute | solution.py:39
  658.3 7.0 %grad_project_out.1 = f32[1024,1024]{1,0:T(8,128)} custom-call(s32[4]{0:T(128)} %pad_add_fusion.2.where_ref, bf16[1024,1024]{1,0:T(8,128)(2,1)} %bitcast.166, bf16[256,1024]{1,0:T(8,128)(2,1)} %copy-done.12, bf16[256,1024]{1,0:T(8,128)(2,1)} %copy-done.21, bf16[256,1024]{1,0:T(8,128)(2,1)} %copy-done.20, bf16[256,1024]{1,0:T(8,128)(2,1)} %copy-done.22), custom_call_target="tpu_custom_call" | custom-call | tf_op jit(solution)/shard_map/grad_project_out/pallas_call | solution.py:509
  673.4 9.7 %conditional.1 = (f32[3,1024,1024]{2,1,0:T(8,128)}) conditional(s32[]{:T(128)} %convert_element_type.91, (s32[]{:T(128)}, bf16[1024,1024]{0,1:T(8,128)(2,1)S(1)}, bf16[3,1024,256]{2,1,0:T(8,128)(2,1)}, bf16[3,1024,256]{2,1,0:T(8,128)(2,1)}, bf16[3,1024,256]{2,1,0:T(8,128)(2,1)}, /*index=5*/bf16[3,1024,256]{2,1,0:T(8,128)(2,1)}) %tuple.68, (s32[]{:T(128)}, ...), branch_computations={%region_2.3_spmd, %region_3.4_spmd} | conditional | bytes 4194312 | solution.py:709
  674.8 8.4 %grad_project_in.3 = f32[3,1024,1024]{2,1,0:T(8,128)} custom-call(s32[1]{0:T(128)} %bitcast.1.ctx_ref, bf16[1024,512]{1,0:T(8,128)(2,1)} %bitcast.170, bf16[3,512,256]{2,1,0:T(8,128)(2,1)} %get-tuple-element.35.refs_0_, bf16[3,512,256]{2,1,0:T(8,128)(2,1)} %get-tuple-element.36.refs_1_, bf16[3,512,256]{2,1,0:T(8,128)(2,1)} %get-tuple-element.37.refs_2_, ...), custom_call_target="tpu_custom_call" | custom-call | tf_op jit(solution)/shard_map/cond/branch_1_fun/grad_project_in/pallas_call | solution.py:482
  (233 shorter events, 196.4 us)
Async XLA Ops:
  7.2 105.9 %all-gather.5.cloned.1.call-start = ((), (), s32[]{:S(2)}) async-start(), calls=%async_computation.6 | async-start | bytes 10485760 | tf_op jit(solution)/shard_map/all_gather | solution.py:623
  7.9 303.3 %collective-permute-start.12 = (bf16[3,1024,1024]{2,1,0:T(8,128)(2,1)}, bf16[3,1024,1024]{2,1,0:T(8,128)(2,1)}, u32[]{:S(2)}, u32[]{:S(2)}) collective-permute-start(bf16[3,1024,1024]{2,1,0:T(8,128)(2,1)} %bitcast.17.weights_ref.refs_0_), channel_id=1, source_target_pairs={{16,18},{17,19},{18,16},{19,17},{20,22},{21,23},{22,20},{23,21},{2... | collective-permute-start | bytes 18874376 | tf_op jit(solution)/shard_map/ppermute | solution.py:39
  11.3 41.3 %collective-permute-start.3 = (bf16[256,1024]{1,0:T(8,128)(2,1)S(1)}, bf16[256,1024]{1,0:T(8,128)(2,1)S(1)}, u32[]{:S(2)}, u32[]{:S(2)}) collective-permute-start(bf16[256,1024]{1,0:T(8,128)(2,1)S(1)} %constant_dynamic-slice_fusion.2), channel_id=1, source_target_pairs={{0,12},{5,1},{10,6},{15,11},{16,4},{21,9},{26,14},{31,3}} | collective-permute-start | bytes 1572872 | tf_op jit(solution)/shard_map/ppermute | solution.py:39
  12.6 40.0 %collective-permute-start.4 = (bf16[256,1024]{1,0:T(8,128)(2,1)S(1)}, bf16[256,1024]{1,0:T(8,128)(2,1)S(1)}, u32[]{:S(2)}, u32[]{:S(2)}) collective-permute-start(bf16[256,1024]{1,0:T(8,128)(2,1)S(1)} %constant_dynamic-slice_fusion.2), channel_id=1, source_target_pairs={{0,8},{5,13},{10,2},{15,7},{16,12},{21,1},{26,6},{31,11}} | collective-permute-start | bytes 1572872 | tf_op jit(solution)/shard_map/ppermute | solution.py:39
  13.9 38.7 %collective-permute-start.5 = (bf16[256,1024]{1,0:T(8,128)(2,1)S(1)}, bf16[256,1024]{1,0:T(8,128)(2,1)S(1)}, u32[]{:S(2)}, u32[]{:S(2)}) collective-permute-start(bf16[256,1024]{1,0:T(8,128)(2,1)S(1)} %constant_dynamic-slice_fusion.2), channel_id=1, source_target_pairs={{0,4},{5,9},{10,14},{15,3},{16,8},{21,13},{26,2},{31,7}} | collective-permute-start | bytes 1572872 | tf_op jit(solution)/shard_map/ppermute | solution.py:39
  122.3 150.8 %collective-permute-start.11 = (bf16[256,1024]{1,0:T(8,128)(2,1)S(1)}, bf16[256,1024]{1,0:T(8,128)(2,1)S(1)}, u32[]{:S(2)}, u32[]{:S(2)}) collective-permute-start(bf16[256,1024]{1,0:T(8,128)(2,1)S(1)} %get-tuple-element.173), channel_id=1, source_target_pairs={{0,28},{4,16},{8,20},{12,24},{1,29},{5,17},{9,21},{13,25},{2,30},{... | collective-permute-start | bytes 1572872 | tf_op jit(solution)/shard_map/ppermute | solution.py:39
  262.7 21.7 %collective-permute-start.10 = (bf16[256,1024]{1,0:T(8,128)(2,1)S(1)}, bf16[256,1024]{1,0:T(8,128)(2,1)S(1)}, u32[]{:S(2)}, u32[]{:S(2)}) collective-permute-start(bf16[256,1024]{1,0:T(8,128)(2,1)S(1)} %get-tuple-element.174), channel_id=1, source_target_pairs={{0,24},{4,28},{8,16},{12,20},{1,25},{5,29},{9,17},{13,21},{2,26},{... | collective-permute-start | bytes 1572872 | tf_op jit(solution)/shard_map/ppermute | solution.py:39
  264.0 31.6 %collective-permute-start.9 = (bf16[256,1024]{1,0:T(8,128)(2,1)S(1)}, bf16[256,1024]{1,0:T(8,128)(2,1)S(1)}, u32[]{:S(2)}, u32[]{:S(2)}) collective-permute-start(bf16[256,1024]{1,0:T(8,128)(2,1)S(1)} %get-tuple-element.175), channel_id=1, source_target_pairs={{0,20},{4,24},{8,28},{12,16},{1,21},{5,25},{9,29},{13,17},{2,22},{... | collective-permute-start | bytes 1572872 | tf_op jit(solution)/shard_map/ppermute | solution.py:39
  265.3 45.3 %collective-permute-start.8 = (bf16[256,1024]{1,0:T(8,128)(2,1)S(1)}, bf16[256,1024]{1,0:T(8,128)(2,1)S(1)}, u32[]{:S(2)}, u32[]{:S(2)}) collective-permute-start(bf16[256,1024]{1,0:T(8,128)(2,1)S(1)} %get-tuple-element.172), channel_id=1, source_target_pairs={{0,16},{4,20},{8,24},{12,28},{1,17},{5,21},{9,25},{13,29},{2,18},{... | collective-permute-start | bytes 1572872 | tf_op jit(solution)/shard_map/ppermute | solution.py:39
  273.1 55.8 %collective-permute-start.19 = (bf16[3,1024,1024]{2,1,0:T(8,128)(2,1)}, bf16[3,1024,1024]{2,1,0:T(8,128)(2,1)}, u32[]{:S(2)}, u32[]{:S(2)}) collective-permute-start(bf16[3,1024,1024]{2,1,0:T(8,128)(2,1)} %bitcast.17.weights_ref.refs_0_), channel_id=1, source_target_pairs={{16,17},{17,16},{18,19},{19,18},{20,21},{21,20},{22,23},{23,22},{2... | collective-permute-start | bytes 18874376 | tf_op jit(solution)/shard_map/ppermute | solution.py:39
  322.9 26.4 %collective-permute-start.2 = (bf16[256,1024]{1,0:T(8,128)(2,1)S(1)}, bf16[256,1024]{1,0:T(8,128)(2,1)S(1)}, u32[]{:S(2)}, u32[]{:S(2)}) collective-permute-start(bf16[256,1024]{1,0:T(8,128)(2,1)S(1)} %collective-permute-done.1), channel_id=1, source_target_pairs={{16,20},{20,24},{24,28},{28,16},{17,21},{21,25},{25,29},{29,17},{1... | collective-permute-start | bytes 1572872 | tf_op jit(solution)/shard_map/ppermute | solution.py:39
  344.4 24.1 %all-to-all-start.2 = ((bf16[4,3,256,256]{3,2,1,0:T(8,128)(2,1)}), bf16[4,3,256,256]{3,2,1,0:T(8,128)(2,1)}, u32[]{:S(2)}, u32[]{:S(2)}) async-start(bf16[4,3,256,256]{3,2,1,0:T(8,128)(2,1)} %get-tuple-element.85), calls=%async_computation.2 | async-start | bytes 3145728 | tf_op jit(solution)/shard_map/all_to_all | solution.py:557
  430.4 112.3 %collective-permute-start.35 = (bf16[3,1024,256]{2,1,0:T(8,128)(2,1)}, bf16[3,1024,256]{2,1,0:T(8,128)(2,1)}, u32[]{:S(2)}, u32[]{:S(2)}) collective-permute-start(bf16[3,1024,256]{2,1,0:T(8,128)(2,1)} %bitcast.60), channel_id=1, source_target_pairs={{16,18},{17,19},{18,16},{19,17},{20,22},{21,23},{22,20},{23,21},{2... | collective-permute-start | bytes 4718600 | tf_op jit(solution)/shard_map/ppermute | solution.py:39
  433.6 66.5 %collective-permute-start.24 = (bf16[256,1024]{1,0:T(8,128)(2,1)}, bf16[256,1024]{1,0:T(8,128)(2,1)}, u32[]{:S(2)}, u32[]{:S(2)}) collective-permute-start(bf16[256,1024]{1,0:T(8,128)(2,1)} %get-tuple-element.165), channel_id=1, source_target_pairs={{16,12},{20,0},{24,4},{28,8},{17,13},{21,1},{25,5},{29,9},{18,14},... | collective-permute-start | bytes 1572872 | tf_op jit(solution)/shard_map/ppermute | solution.py:39
  434.9 97.4 %collective-permute-start.23 = (bf16[256,1024]{1,0:T(8,128)(2,1)}, bf16[256,1024]{1,0:T(8,128)(2,1)}, u32[]{:S(2)}, u32[]{:S(2)}) collective-permute-start(bf16[256,1024]{1,0:T(8,128)(2,1)} %get-tuple-element.166), channel_id=1, source_target_pairs={{16,8},{20,12},{24,0},{28,4},{17,9},{21,13},{25,1},{29,5},{18,10},... | collective-permute-start | bytes 1572872 | tf_op jit(solution)/shard_map/ppermute | solution.py:39
  436.2 97.5 %collective-permute-start.22 = (bf16[256,1024]{1,0:T(8,128)(2,1)}, bf16[256,1024]{1,0:T(8,128)(2,1)}, u32[]{:S(2)}, u32[]{:S(2)}) collective-permute-start(bf16[256,1024]{1,0:T(8,128)(2,1)} %get-tuple-element.167), channel_id=1, source_target_pairs={{16,4},{20,8},{24,12},{28,0},{17,5},{21,9},{25,13},{29,1},{18,6},{... | collective-permute-start | bytes 1572872 | tf_op jit(solution)/shard_map/ppermute | solution.py:39
  437.5 96.5 %collective-permute-start.21 = (bf16[256,1024]{1,0:T(8,128)(2,1)}, bf16[256,1024]{1,0:T(8,128)(2,1)}, u32[]{:S(2)}, u32[]{:S(2)}) collective-permute-start(bf16[256,1024]{1,0:T(8,128)(2,1)} %get-tuple-element.164), channel_id=1, source_target_pairs={{16,0},{20,4},{24,8},{28,12},{17,1},{21,5},{25,9},{29,13},{18,2},{... | collective-permute-start | bytes 1572872 | tf_op jit(solution)/shard_map/ppermute | solution.py:39
  500.1 40.8 %collective-permute-start.33 = (bf16[256,1024]{1,0:T(8,128)(2,1)S(1)}, bf16[256,1024]{1,0:T(8,128)(2,1)}, u32[]{:S(2)}, u32[]{:S(2)}) collective-permute-start(bf16[256,1024]{1,0:T(8,128)(2,1)S(1)} %get-tuple-element.161), channel_id=1, source_target_pairs={{16,19},{17,18},{18,17},{19,16},{20,23},{21,22},{22,21},{23,20},{2... | collective-permute-start | bytes 1572872 | tf_op jit(solution)/shard_map/ppermute | solution.py:39
  541.0 42.2 %collective-permute-start.34 = (bf16[3,1024,256]{2,1,0:T(8,128)(2,1)}, bf16[3,1024,256]{2,1,0:T(8,128)(2,1)}, u32[]{:S(2)}, u32[]{:S(2)}) collective-permute-start(bf16[3,1024,256]{2,1,0:T(8,128)(2,1)} %bitcast.60), channel_id=1, source_target_pairs={{16,17},{17,16},{18,19},{19,18},{20,21},{21,20},{22,23},{23,22},{2... | collective-permute-start | bytes 4718600 | tf_op jit(solution)/shard_map/ppermute | solution.py:39
  542.8 40.4 %collective-permute-start.36 = (bf16[3,1024,256]{2,1,0:T(8,128)(2,1)}, bf16[3,1024,256]{2,1,0:T(8,128)(2,1)}, u32[]{:S(2)}, u32[]{:S(2)}) collective-permute-start(bf16[3,1024,256]{2,1,0:T(8,128)(2,1)} %collective-permute-done.35), channel_id=1, source_target_pairs={{16,17},{17,16},{18,19},{19,18},{20,21},{21,20},{22,23},{23,22},{2... | collective-permute-start | bytes 4718600 | tf_op jit(solution)/shard_map/ppermute | solution.py:39
  603.9 53.0 %all-to-all-start.5 = ((bf16[4,256,1024]{2,1,0:T(8,128)(2,1)}), bf16[4,256,1024]{2,1,0:T(8,128)(2,1)S(1)}, u32[]{:S(2)}, u32[]{:S(2)}) async-start(bf16[4,256,1024]{2,1,0:T(8,128)(2,1)} %pad_maximum_fusion.6), calls=%async_computation.5 | async-start | bytes 4194304 | tf_op jit(solution)/shard_map/all_to_all | solution.py:557
  617.6 47.6 %collective-permute-start.41 = (bf16[3,512,256]{2,1,0:T(8,128)(2,1)}, bf16[3,512,256]{2,1,0:T(8,128)(2,1)}, u32[]{:S(2)}, u32[]{:S(2)}) collective-permute-start(bf16[3,512,256]{2,1,0:T(8,128)(2,1)} %get-tuple-element.105), channel_id=1, source_target_pairs={{0,2},{1,3},{2,0},{3,1},{4,6},{5,7},{6,4},{7,5},{8,10},{9,11},{10,... | collective-permute-start | bytes 2359304 | tf_op jit(solution)/shard_map/ppermute | solution.py:39
  623.5 29.9 %collective-permute-start.44 = (f32[138,256]{1,0:T(8,128)}, f32[138,256]{1,0:T(8,128)}, u32[]{:S(2)}, u32[]{:S(2)}) collective-permute-start(f32[138,256]{1,0:T(8,128)} %pad_maximum_fusion.10), channel_id=1, source_target_pairs={{0,2},{1,3},{2,0},{3,1},{16,18},{17,19},{18,16},{19,17},{4,6},{5,7... | collective-permute-start | bytes 423944 | tf_op jit(solution)/shard_map/ppermute | solution.py:39
  623.5 44.1 %collective-permute-start.43 = (f32[138,256]{1,0:T(8,128)}, f32[138,256]{1,0:T(8,128)}, u32[]{:S(2)}, u32[]{:S(2)}) collective-permute-start(f32[138,256]{1,0:T(8,128)} %pad_maximum_fusion.10), channel_id=1, source_target_pairs={{0,1},{1,0},{2,3},{3,2},{16,17},{17,16},{18,19},{19,18},{4,5},{5,4... | collective-permute-start | bytes 423944 | tf_op jit(solution)/shard_map/ppermute | solution.py:39
  (61 other events, 807.5 us)
Sparse Core Ops, SparseCore 0:
  9.6 61.2 all-gather.4
